TPU v7x, 32 devices: a whole 2x2x4 slice. The times are simulated.
32 devices in a mesh: rep: 2 (over y), grp: 2 (over core), blk: 8 (over z, x).
Axes of the slice: x: 2, y: 2, z: 4, core: 2. Of those that a mesh axis runs over, the one named last changes fastest.
Arguments:
- queries: bfloat16 [2048, 8, 576], P(('rep', 'grp'), 'blk'), parts along dimension 0, may hold values from -64 to 64
- latents: bfloat16 [2048, 576], P(('rep', 'grp', 'blk')), parts along dimension 0, may hold values from -12 to 12
- out_grad: bfloat16 [2048, 8, 512], P(('rep', 'grp'), 'blk'), parts along dimension 0, may hold values from -6 to 6
- first_key: int32 [2048], P(('rep', 'grp')), parts along dimension 0, may hold values from 0 to 127, as said below
Outputs:
- query_grad: bfloat16 [2048, 8, 576], P(('rep', 'grp'), 'blk'), parts along dimension 0
- latent_grad: bfloat16 [2048, 576], P(('rep', 'grp', 'blk')), parts along dimension 0
There are 2 independent parts, one for each index of `rep`. A program takes and returns all parts, laid end to end along the dimension named above; each array names one. Nothing has to cross between parts.
Inputs may be any that keep to these rules, and one draw needn't show every extreme that they name: `first_key`: 0 for tokens of the first block; for a token of block b >= 1 a position among the first 128 of block b - 1.
All inputs are finite; a program needn't handle non-finite values.
Results may differ from a plain program's by a relative error of at most 0.0055.
Values may be sent and summed in bfloat16 or wider, within the bound.
A program may use at most 64 MiB of HBM per device.

v0:
```python
import jax
import jax.numpy as jnp
from jax import lax
from jax.sharding import PartitionSpec as P

score_scale = 192.0 ** (-0.5)


def shifted(shard, axis, by):
    count = lax.axis_size(axis)
    pairs = [(i, i + by) for i in range(count) if 0 <= i + by < count]
    return lax.ppermute(shard, axis, pairs)


def attend_grads(query_blk, grad_blk, key_rows, visible):
    count, head_count, width = query_blk.shape
    query_rows = query_blk.reshape(count * head_count, width)
    grad_rows = grad_blk.reshape(count * head_count, -1)
    rank_width = grad_rows.shape[1]
    value_rows = key_rows[:, :rank_width]
    scores = jnp.dot(query_rows, key_rows.T, preferred_element_type=jnp.float32) * score_scale
    scores = scores.reshape(count, head_count, -1)
    mask_three = visible[:, None, :]
    row_max = jnp.max(jnp.where(mask_three, scores, -jnp.inf), axis=-1, keepdims=True)
    total = jnp.sum(jnp.where(mask_three, jnp.exp(scores - row_max), 0.0), axis=-1, keepdims=True)
    log_norm = row_max + jnp.log(total)
    attn_probs = jnp.where(mask_three, jnp.exp(scores - log_norm), 0.0).astype(jnp.bfloat16)
    attn_probs = attn_probs.reshape(count * head_count, -1)
    outputs = jnp.dot(attn_probs, value_rows, preferred_element_type=jnp.float32)
    row_delta = jnp.sum(grad_rows.astype(jnp.float32) * outputs, axis=-1, keepdims=True)
    prob_grad = jnp.dot(grad_rows, value_rows.T, preferred_element_type=jnp.float32)
    score_grad = (attn_probs.astype(jnp.float32) * (prob_grad - row_delta) * score_scale).astype(
        jnp.bfloat16
    )
    query_grad = jnp.dot(score_grad, key_rows, preferred_element_type=jnp.float32).astype(
        jnp.bfloat16
    )
    latent_part = jnp.dot(score_grad.T, query_rows, preferred_element_type=jnp.float32)
    value_part = jnp.dot(attn_probs.T, grad_rows, preferred_element_type=jnp.float32)
    latent_part = jnp.concatenate(
        [latent_part[:, :rank_width] + value_part, latent_part[:, rank_width:]], axis=1
    )
    return (query_grad.reshape(count, head_count, width), latent_part)


def shards(queries, latents, out_grad, first_key):
    block_len = queries.shape[0]
    head_local = queries.shape[1]
    width = queries.shape[2]
    rank_width = out_grad.shape[2]
    group_index = lax.axis_index("grp")
    own_block = lax.all_gather(latents, "blk", axis=0, tiled=True)
    prev_block = shifted(own_block, "grp", 1)
    key_rows = jnp.concatenate([prev_block, own_block], axis=0)
    key_iota = jnp.arange(2 * block_len, dtype=jnp.int32)
    key_pos = key_iota + (group_index - 1) * block_len
    in_prev = key_iota < block_len
    piece = min(512, block_len)
    pieces = block_len // piece
    query_steps = queries.reshape(pieces, piece, head_local, width)
    grad_steps = out_grad.reshape(pieces, piece, head_local, rank_width)
    first_steps = first_key.reshape(pieces, piece)
    pos_steps = (jnp.arange(block_len, dtype=jnp.int32) + group_index * block_len).reshape(
        pieces, piece
    )

    def scan_step(carry, items):
        query_blk, grad_blk, first_blk, pos_blk = items
        prev_ok = (key_pos[None, :] >= first_blk[:, None]) & (group_index > 0)
        own_ok = key_pos[None, :] <= pos_blk[:, None]
        visible = jnp.where(in_prev[None, :], prev_ok, own_ok)
        query_part, latent_part = attend_grads(query_blk, grad_blk, key_rows, visible)
        return (carry + latent_part, query_part)

    carry_init = jnp.zeros((2 * block_len, width), jnp.float32)
    latent_part, query_blocks = lax.scan(
        scan_step, carry_init, (query_steps, grad_steps, first_steps, pos_steps)
    )
    query_grad = query_blocks.reshape(block_len, head_local, width)
    prev_part = latent_part[:block_len]
    own_part = latent_part[block_len:]
    from_later = shifted(prev_part.astype(jnp.bfloat16), "grp", -1).astype(prev_part.dtype)
    latent_total = lax.psum_scatter(own_part + from_later, "blk", scatter_dimension=0, tiled=True)
    return (query_grad, latent_total.astype(jnp.bfloat16))


def solution(mesh):
    placed = (
        P(("rep", "grp"), "blk", None),
        P(("rep", "grp", "blk"), None),
        P(("rep", "grp"), "blk", None),
        P(("rep", "grp")),
    )
    return jax.shard_map(
        shards,
        mesh=mesh,
        in_specs=placed,
        out_specs=(P(("rep", "grp"), "blk", None), P(("rep", "grp", "blk"), None)),
        check_vma=False,
    )
```

profile of v0, /device:TPU:0, one launch (start us, length us, event | category | flops | bytes accessed | tf_op | source)
XLA Modules:
  0.0 131.3 jit_solution(18271201214269916155)
XLA Ops:
  7.2 0.0 reduce-scatter.4.cloned.1.call-start
  7.2 33.8 %all_gather.3 = bf16[512,576]{1,0:T(8,128)(2,1)S(1)} all-gather(bf16[64,576]{1,0:T(8,128)(2,1)} %param.5), channel_id=1, replica_groups=mesh['rep'=2,'grp'=2,'blk'=8] {'blk'}, dimensions={0}, use_global_device_ids=true | all-gather | bytes 663552 | tf_op jit(solution)/shard_map/all_gather | solution.py:52
  41.0 0.2 copy.11
  41.3 1.3 %collective-permute-start = (bf16[512,576]{0,1:T(8,128)(2,1)S(1)}, bf16[512,576]{0,1:T(8,128)(2,1)S(1)}, u32[]{:S(2)}, u32[]{:S(2)}) collective-permute-start(bf16[512,576]{0,1:T(8,128)(2,1)S(1)} %copy.11), channel_id=1, source_target_pairs={{0,8},{1,9},{2,10},{3,11},{4,12},{5,13},{6,14},{7,15},{16,24},{17,... | collective-permute-start | bytes 1769480 | tf_op jit(solution)/shard_map/ppermute | solution.py:12
  42.6 1.0 copy.13
  43.6 0.5 collective-permute-done
  44.2 0.3 copy.12
  44.5 1.4 %fusion.2 = (f32[512]{0:T(512)S(1)}, f32[1024,512]{1,0:T(8,128)S(1)}) fusion(s32[512]{0:T(512)S(1)} %iota_add_fusion.1, pred[]{:T(512)S(6)} %gt.4, s32[512]{0:T(512)S(1)} %copy-done.4, s32[1024]{0:T(1024)S(1)} %iota_add_fusion, pred[1024]{0:T(1024)(128)(4,1)S(1)} %iota_compare_fusion, bf16[512,1,576]{0,2,1:T(8,128)(2,1)S(1)} %copy-done, ...), kind=kOutput, calls=%fused_computation.9 | convolution fusion | flops 610008576 | bytes 3877889 | tf_op jit(solution)/shard_map/while/body/eval_jaxpr/dot_general | solution.py:21
  45.9 1.2 fusion.5
  47.1 1.2 fusion.8
  48.3 0.8 fusion.10
  49.1 0.8 fusion.1
  49.9 0.8 fusion.15
  50.7 0.8 slice_add_fusion
  51.6 0.1 fusion.13
  51.6 1.3 collective-permute-start.1
  52.9 2.6 %collective-permute-done.1 = bf16[512,576]{0,1:T(8,128)(2,1)S(1)} collective-permute-done((bf16[512,576]{0,1:T(8,128)(2,1)S(1)}, bf16[512,576]{0,1:T(8,128)(2,1)S(1)}, u32[]{:S(2)}, u32[]{:S(2)}) %collective-permute-start.1) | collective-permute-done | bytes 589856 | tf_op jit(solution)/shard_map/ppermute | solution.py:12
  55.5 0.2 fusion.12
  55.7 1.5 %copy.15 = f32[512,576]{1,0:T(8,128)} copy(f32[512,576]{0,1:T(8,128)S(1)} %fusion.12) | data formatting | bytes 2359296
  57.2 0.0 reduce-scatter.4.cloned.1.call-update
  57.2 2.7 %fusion.9 = bf16[512,1,576]{0,2,1:T(8,128)(2,1)} fusion(bf16[512,1024]{0,1:T(8,128)(2,1)S(1)} %fusion.1, bf16[512,576]{1,0:T(8,128)(2,1)S(1)} %all_gather.3, bf16[512,576]{1,0:T(8,128)(2,1)} %copy-done.2), kind=kOutput, calls=%fused_computation.20 | convolution fusion | flops 606633984 | bytes 2818048 | tf_op jit(solution)/shard_map/while/body/eval_jaxpr/dot_general | solution.py:35
  60.0 62.7 %reduce-scatter.4.cloned.1.call-done = f32[64,576]{1,0:T(8,128)} async-done(((f32[512,576]{1,0:T(8,128)}), f32[64,576]{1,0:T(8,128)}) %reduce-scatter.4.cloned.1.call-update) | async-done | bytes 147472
  122.6 1.0 copy.16
  123.7 0.8 copy.14
  (15 shorter events, 0.1 us)
Async XLA Ops:
  7.2 37.3 %copy-start = (bf16[512,1,576]{0,2,1:T(8,128)(2,1)S(1)}, bf16[512,1,576]{0,2,1:T(8,128)(2,1)}, u32[]{:S(2)}) copy-start(bf16[512,1,576]{0,2,1:T(8,128)(2,1)} %param.4) | copy-start | bytes 1769476
  7.2 35.4 %copy-start.1 = (bf16[512,1,512]{2,0,1:T(8,128)(2,1)S(1)}, bf16[512,1,512]{2,0,1:T(8,128)(2,1)}, u32[]{:S(2)}) copy-start(bf16[512,1,512]{2,0,1:T(8,128)(2,1)} %param.6) | copy-start | bytes 1572868
  7.2 37.3 %copy-start.4 = (s32[512]{0:T(512)S(1)}, s32[512]{0:T(512)}, u32[]{:S(2)}) copy-start(s32[512]{0:T(512)} %param.7) | copy-start | bytes 6148
  7.2 115.4 %reduce-scatter.4.cloned.1.call-start = ((), (), s32[]{:S(2)}) async-start(), calls=%async_computation.1 | async-start | bytes 1474560
  41.3 2.9 %collective-permute-start = (bf16[512,576]{0,1:T(8,128)(2,1)S(1)}, bf16[512,576]{0,1:T(8,128)(2,1)S(1)}, u32[]{:S(2)}, u32[]{:S(2)}) collective-permute-start(bf16[512,576]{0,1:T(8,128)(2,1)S(1)} %copy.11), channel_id=1, source_target_pairs={{0,8},{1,9},{2,10},{3,11},{4,12},{5,13},{6,14},{7,15},{16,24},{17,... | collective-permute-start | bytes 1769480 | tf_op jit(solution)/shard_map/ppermute | solution.py:12
  44.5 4.6 %copy-start.2 = (bf16[512,576]{1,0:T(8,128)(2,1)}, bf16[512,576]{1,0:T(8,128)(2,1)S(1)}, u32[]{:S(2)}) copy-start(bf16[512,576]{1,0:T(8,128)(2,1)S(1)} %copy.12) | copy-start | bytes 1769476
  47.1 1.2 copy-start.3
  51.6 3.9 %collective-permute-start.1 = (bf16[512,576]{0,1:T(8,128)(2,1)S(1)}, bf16[512,576]{0,1:T(8,128)(2,1)S(1)}, u32[]{:S(2)}, u32[]{:S(2)}) collective-permute-start(bf16[512,576]{0,1:T(8,128)(2,1)S(1)} %fusion.13), channel_id=1, source_target_pairs={{8,0},{9,1},{10,2},{11,3},{12,4},{13,5},{14,6},{15,7},{24,16},{25,... | collective-permute-start | bytes 1769480 | tf_op jit(solution)/shard_map/ppermute | solution.py:12
Sparse Core Ops, SparseCore 0:
  57.4 65.2 reduce-scatter.3
where the time goes:
time: 132 us; the launch traced here: 131 us
  waiting for transfers between devices  65.8 us (50%)
  blocking collectives  33.8 us (26%)
  between operations  14.2 us (11%)
  matrix products  7.27 us (6%)
  local copies, waits for them, and re-layouts  4.87 us (4%)
  other arithmetic  2.68 us (2%)
  starting transfers between devices  2.66 us (2%)
    unnamed x2, waiting for transfers between devices  62.7 us
    all_gather x1, blocking collectives, shards(): own_block = lax.all_gather(latents, 'blk', axis=0, tiled=True)  33.8 us
    unnamed x14, local copies, waits for them, and re-layouts  4.32 us
    ppermute x2, waiting for transfers between devices, shifted(): return lax.ppermute(shard, axis, pairs)  3.14 us
    dot_general x1, matrix products, attend_grads(): jnp.dot(score_grad, key_rows, preferred_element_type=jnp.float32)  2.73 us
  transfers between devices with their start and end apart: 3, of which 3 were waited for; matrix products, arithmetic and copies ran while one was open for 3% of the time, Pallas kernels for 0%

commit v1 on v0

--- a/solution.py
+++ b/solution.py
@@ -1,6 +1,10 @@
+import functools
+
 import jax
 import jax.numpy as jnp
 from jax import lax
+from jax.experimental import pallas as pl
+from jax.experimental.pallas import tpu as pltpu
 from jax.sharding import PartitionSpec as P
 
 score_scale = 192.0 ** (-0.5)
@@ -43,7 +47,7 @@
     return (query_grad.reshape(count, head_count, width), latent_part)
 
 
-def shards(queries, latents, out_grad, first_key):
+def shards_by_collectives(queries, latents, out_grad, first_key):
     block_len = queries.shape[0]
     head_local = queries.shape[1]
     width = queries.shape[2]
@@ -84,6 +88,334 @@
     return (query_grad, latent_total.astype(jnp.bfloat16))
 
 
+MESH = pl.DeviceIdType.MESH
+TILE = 128
+HIDDEN = -1e30
+
+
+def xor(a, b, count):
+    out, bit = 0, 1
+    while bit < count:
+        out = out + bit * ((a // bit + b // bit) % 2)
+        bit *= 2
+    return out
+
+
+def dot_nt(a, b):
+    return lax.dot_general(a, b, (((1,), (1,)), ((), ())), preferred_element_type=jnp.float32)
+
+
+def dot_tn(a, b):
+    return lax.dot_general(a, b, (((0,), (0,)), ((), ())), preferred_element_type=jnp.float32)
+
+
+def dot_nn(a, b):
+    return jnp.dot(a, b, preferred_element_type=jnp.float32)
+
+
+def kernel(
+    groups, count, q_hbm, lat_hbm, grad_hbm, first_ref, dq_hbm, dl_ref,
+    q, grad, kv, s, dp, p, ds, dq, acc, own_acc, part, red, prev_part, next_part,
+    in_sem, gat_send, gat_recv, fwd_send, fwd_recv, pp_send, pp_recv, red_send, red_recv, out_sem,
+):
+    width, block = q.shape
+    rank = grad.shape[1]
+    rows = block // count
+    tiles = block // TILE
+    per_tile = TILE // rows
+    me = lax.axis_index("blk")
+    group = lax.axis_index("grp")
+    has_prev = group > 0
+    has_next = group < groups - 1
+    my_tile = me // per_tile
+    prev_tiles = tiles * jnp.minimum(group, 1)
+
+    barrier = pltpu.get_barrier_semaphore()
+    for d in range(1, count):
+        pl.semaphore_signal(barrier, inc=1, device_id={"blk": xor(me, d, count)}, device_id_type=MESH)
+
+    @pl.when(has_prev)
+    def _():
+        pl.semaphore_signal(barrier, inc=1, device_id={"grp": group - 1}, device_id_type=MESH)
+
+    @pl.when(has_next)
+    def _():
+        pl.semaphore_signal(barrier, inc=1, device_id={"grp": group + 1}, device_id_type=MESH)
+
+    own_shard = pltpu.make_async_copy(lat_hbm, kv.at[pl.ds(block + me * rows, rows)], in_sem.at[0])
+    q_copy = pltpu.make_async_copy(q_hbm, q, in_sem.at[1])
+    grad_copy = pltpu.make_async_copy(grad_hbm, grad, in_sem.at[2])
+    own_shard.start()
+    q_copy.start()
+    grad_copy.start()
+
+    if groups == 2:
+        pl.semaphore_wait(barrier, count)
+    else:
+        ends = jnp.minimum(group, 1) + jnp.minimum(groups - 1 - group, 1)
+        pl.semaphore_wait(barrier, count - 1 + ends)
+
+    def gather(d, source, target):
+        return pltpu.make_async_remote_copy(
+            src_ref=lat_hbm,
+            dst_ref=kv.at[pl.ds(block + source * rows, rows)],
+            send_sem=gat_send.at[d],
+            recv_sem=gat_recv.at[source],
+            device_id={"blk": target},
+            device_id_type=MESH,
+        )
+
+    def forward(j, to):
+        return pltpu.make_async_remote_copy(
+            src_ref=kv.at[pl.ds(block + j * rows, rows)],
+            dst_ref=kv.at[pl.ds(j * rows, rows)],
+            send_sem=fwd_send.at[j],
+            recv_sem=fwd_recv.at[j],
+            device_id={"grp": to},
+            device_id_type=MESH,
+        )
+
+    def prev_terms(tile, to):
+        return pltpu.make_async_remote_copy(
+            src_ref=prev_part.at[pl.ds(tile * TILE, TILE)],
+            dst_ref=next_part.at[pl.ds(tile * TILE, TILE)],
+            send_sem=pp_send.at[tile],
+            recv_sem=pp_recv.at[tile],
+            device_id={"grp": to},
+            device_id_type=MESH,
+        )
+
+    def reduce(source, target):
+        return pltpu.make_async_remote_copy(
+            src_ref=part.at[pl.ds(target * rows, rows)],
+            dst_ref=red.at[source],
+            send_sem=red_send.at[target],
+            recv_sem=red_recv.at[source],
+            device_id={"blk": target},
+            device_id_type=MESH,
+        )
+
+    for d in range(count - 1, 0, -1):
+        gather(d, me, xor(me, d, count)).start()
+    own_shard.wait()
+    q_copy.wait()
+    grad_copy.wait()
+
+    key_in_tile = lax.broadcasted_iota(jnp.int32, (TILE, block), 0)
+    token = lax.broadcasted_iota(jnp.int32, (TILE, block), 1)
+
+    def scores_of(start, visible, largest):
+        at = pl.ds(pl.multiple_of(start, TILE), TILE)
+        keys = kv[at, :]
+        tile_s = jnp.where(visible, dot_nn(keys, q[...]) * score_scale, HIDDEN)
+        s[at, :] = tile_s
+        dp[at, :] = dot_nt(keys[:, :rank], grad[...])
+        return jnp.maximum(largest, jnp.max(tile_s, axis=0, keepdims=True))
+
+    def own_scores(step, largest):
+        tile = xor(my_tile, step, tiles)
+        for sub in range(per_tile):
+            j = tile * per_tile + sub
+
+            @pl.when(j != me)
+            def _():
+                gather(0, j, j).wait_recv()
+
+            @pl.when(has_next)
+            def _():
+                forward(j, group + 1).start()
+
+        return scores_of(block + tile * TILE, tile * TILE + key_in_tile <= token, largest)
+
+    def prev_scores(step, largest):
+        tile = xor(my_tile, step, tiles)
+        for sub in range(per_tile):
+            forward(tile * per_tile + sub, group - 1).wait_recv()
+        position = (group - 1) * block + tile * TILE + key_in_tile
+        return scores_of(tile * TILE, position >= first_ref[...], largest)
+
+    largest = jnp.full((1, block), HIDDEN, jnp.float32)
+    largest = lax.fori_loop(0, tiles, own_scores, largest)
+    largest = lax.fori_loop(0, prev_tiles, prev_scores, largest)
+
+    def tile_rows(i):
+        return pl.ds(pl.multiple_of(i * TILE, TILE), TILE)
+
+    def exps(i, total):
+        at = tile_rows(i)
+        e = jnp.exp(s[at, :] - largest)
+        s[at, :] = e
+        return total + jnp.sum(e, axis=0, keepdims=True)
+
+    zero = jnp.zeros((1, block), jnp.float32)
+    first_tile = tiles - prev_tiles
+    inverse = 1.0 / lax.fori_loop(first_tile, 2 * tiles, exps, zero)
+
+    def probs(i, delta):
+        at = tile_rows(i)
+        tile_p = (s[at, :] * inverse).astype(jnp.bfloat16)
+        p[at, :] = tile_p
+        return delta + jnp.sum(tile_p.astype(jnp.float32) * dp[at, :], axis=0, keepdims=True)
+
+    delta = lax.fori_loop(first_tile, 2 * tiles, probs, zero)
+
+    def score_grads(i, carry):
+        at = tile_rows(i)
+        ds[at, :] = (p[at, :].astype(jnp.float32) * (dp[at, :] - delta) * score_scale).astype(jnp.bfloat16)
+        return carry
+
+    lax.fori_loop(first_tile, 2 * tiles, score_grads, 0)
+
+    def latent_terms(start):
+        at = pl.ds(pl.multiple_of(start, TILE), TILE)
+        d = ds[at, :]
+        acc[...] = dot_nt(d, q[...])
+        acc[:, :rank] += dot_nn(p[at, :], grad[...])
+
+    def prev_latents(step, carry):
+        tile = xor(my_tile, tiles - 1 - step, tiles)
+        latent_terms(tile * TILE)
+        prev_part[pl.ds(pl.multiple_of(tile * TILE, TILE), TILE), :] = acc[...].astype(jnp.bfloat16)
+        prev_terms(tile, group - 1).start()
+        return carry
+
+    lax.fori_loop(0, prev_tiles, prev_latents, 0)
+
+    def query_grads():
+        for start in range(0, block, 256):
+            cut = slice(start, min(start + 256, block))
+
+            @pl.when(has_prev)
+            def _():
+                dq[:, cut] = dot_tn(kv[...], ds[:, cut]).astype(jnp.bfloat16)
+
+            @pl.when(group == 0)
+            def _():
+                dq[:, cut] = dot_tn(kv[block:, :], ds[block:, cut]).astype(jnp.bfloat16)
+
+        pltpu.make_async_copy(dq, dq_hbm, out_sem).start()
+
+    @pl.when(has_next)
+    def _():
+        query_grads()
+
+    def own_latents(step, carry):
+        tile = xor(my_tile, tiles - 1 - step, tiles)
+        at = pl.ds(pl.multiple_of(tile * TILE, TILE), TILE)
+        latent_terms(block + tile * TILE)
+
+        @pl.when(has_next)
+        def _():
+            prev_terms(tile, group + 1).wait_recv()
+            acc[...] += next_part[at, :].astype(jnp.float32)
+
+        part[at, :] = acc[...].astype(jnp.bfloat16)
+        for sub in range(per_tile):
+            j = tile * per_tile + sub
+
+            @pl.when(j != me)
+            def _():
+                reduce(me, j).start()
+
+            @pl.when(j == me)
+            def _():
+                own_acc[...] = acc[sub * rows:(sub + 1) * rows, :]
+
+        return carry
+
+    lax.fori_loop(0, tiles, own_latents, 0)
+
+    @pl.when(group == groups - 1)
+    def _():
+        query_grads()
+
+    total = own_acc[...]
+    for d in range(1, count):
+        source = xor(me, d, count)
+        reduce(source, me).wait_recv()
+        total = total + red[source].astype(jnp.float32)
+    dl_ref[...] = total.astype(dl_ref.dtype)
+
+    pltpu.make_async_copy(dq, dq_hbm, out_sem).wait()
+    for d in range(1, count):
+        gather(d, me, xor(me, d, count)).wait_send()
+        reduce(me, xor(me, d, count)).wait_send()
+
+    @pl.when(has_next)
+    def _():
+        for j in range(count):
+            forward(j, group + 1).wait_send()
+
+    @pl.when(has_prev)
+    def _():
+        for tile in range(tiles):
+            prev_terms(tile, group - 1).wait_send()
+
+
+def fits(count, block, head_local):
+    rows = block // count
+    tiles = block // TILE
+    powers = count & (count - 1) == 0 and tiles & (tiles - 1) == 0
+    return head_local == 1 and rows % 16 == 0 and TILE % rows == 0 and block % TILE == 0 and powers
+
+
+def shards(queries, latents, out_grad, first_key):
+    block, head_local, width = queries.shape
+    rank = out_grad.shape[2]
+    count, groups = lax.axis_size("blk"), lax.axis_size("grp")
+    if not fits(count, block, head_local):
+        return shards_by_collectives(queries, latents, out_grad, first_key)
+    rows, tiles = block // count, block // TILE
+    bf16, f32 = jnp.bfloat16, jnp.float32
+    dma = pltpu.SemaphoreType.DMA
+    anywhere = pl.BlockSpec(memory_space=pl.ANY)
+    vmem = pl.BlockSpec(memory_space=pltpu.VMEM)
+    query_grad, latent_grad = pl.pallas_call(
+        functools.partial(kernel, groups, count),
+        out_shape=(
+            jax.ShapeDtypeStruct((width, block), bf16),
+            jax.ShapeDtypeStruct((rows, width), bf16),
+        ),
+        in_specs=[anywhere, anywhere, anywhere, vmem],
+        out_specs=(anywhere, vmem),
+        scratch_shapes=[
+            pltpu.VMEM((width, block), bf16),
+            pltpu.VMEM((block, rank), bf16),
+            pltpu.VMEM((2 * block, width), bf16),
+            pltpu.VMEM((2 * block, block), f32),
+            pltpu.VMEM((2 * block, block), f32),
+            pltpu.VMEM((2 * block, block), bf16),
+            pltpu.VMEM((2 * block, block), bf16),
+            pltpu.VMEM((width, block), bf16),
+            pltpu.VMEM((TILE, width), f32),
+            pltpu.VMEM((rows, width), f32),
+            pltpu.VMEM((block, width), bf16),
+            pltpu.VMEM((count, rows, width), bf16),
+            pltpu.VMEM((block, width), bf16),
+            pltpu.VMEM((block, width), bf16),
+            dma((3,)),
+            dma((count,)),
+            dma((count,)),
+            dma((count,)),
+            dma((count,)),
+            dma((tiles,)),
+            dma((tiles,)),
+            dma((count,)),
+            dma((count,)),
+            dma,
+        ],
+        compiler_params=pltpu.CompilerParams(
+            collective_id=0, has_side_effects=True, vmem_limit_bytes=40 * 1024 * 1024
+        ),
+    )(
+        queries.reshape(block, width).T,
+        latents,
+        out_grad.reshape(block, rank),
+        first_key.reshape(1, block),
+    )
+    return (query_grad.T.reshape(block, 1, width), latent_grad)
+
+
 def solution(mesh):
     placed = (
         P(("rep", "grp"), "blk", None),

time: 132 us -> 45.4 us (0.34)
  waiting for transfers between devices: 65.8 us -> 0 us
  Pallas kernels: 0 us -> 38.8 us
  blocking collectives: 33.8 us -> 0 us
  between operations: 14.2 us -> 0.65 us
  matrix products: 7.27 us -> 0 us
  other arithmetic: 2.68 us -> 0 us
  starting transfers between devices: 2.66 us -> 0 us
    unnamed x2 -> x0, waiting for transfers between devices: 62.7 us -> none
    pallas_call x0 -> x1, Pallas kernels: none -> 38.8 us  [shards(): pl.pallas_call(functools.partial(kernel, groups, count), out_shape=(jax.S...]
    all_gather x1 -> x0, blocking collectives: 33.8 us -> none  [shards(): own_block = lax.all_gather(latents, 'blk', axis=0, tiled=True)]
    dot_general x6 -> x0, matrix products: 7.27 us -> none  [the longest x1 2.73 us: attend_grads(): jnp.dot(score_grad, key_rows, preferred_element_type=jnp.float32)]
    ppermute x2 -> x0, waiting for transfers between devices: 3.14 us -> none  [shifted(): return lax.ppermute(shard, axis, pairs)]
    ppermute x2 -> x0, starting transfers between devices: 2.62 us -> none  [shifted(): return lax.ppermute(shard, axis, pairs)]
    unnamed x14 -> x10, local copies, waits for them, and re-layouts: 4.32 us -> 5.12 us
  transfers between devices with their start and end apart: 3 -> 0, of which waited for: 3 -> 0; matrix products, arithmetic and copies ran while one was open for 3% -> 0% of each run, Pallas kernels for 0% -> 0%
where the time goes in v1:
time: 45.4 us; the launch traced here: 44.6 us
  Pallas kernels  38.8 us (85%)
  local copies, waits for them, and re-layouts  5.12 us (11%)
  between operations  0.65 us (1%)
    pallas_call x1, Pallas kernels, shards(): pl.pallas_call(functools.partial(kernel, groups, count), out_shape=(jax.S...  38.8 us
    unnamed x10, local copies, waits for them, and re-layouts  5.12 us

profile of v1, /device:TPU:0, one launch (start us, length us, event | category | flops | bytes accessed | tf_op | source)
XLA Modules:
  0.0 44.6 jit_solution(537025786678616422)
XLA Ops:
  0.6 0.0 copy-start.3
  0.6 0.7 %copy-done.3 = s32[512]{0:T(512)S(1)} copy-done((s32[512]{0:T(512)S(1)}, s32[512]{0:T(512)}, u32[]{:S(2)}) %copy-start.3) | copy-done | bytes 2072
  1.3 0.0 copy-start
  1.3 1.1 %copy-done = bf16[512,1,576]{0,2,1:T(8,128)(2,1)S(1)} copy-done((bf16[512,1,576]{0,2,1:T(8,128)(2,1)S(1)}, bf16[512,1,576]{0,2,1:T(8,128)(2,1)}, u32[]{:S(2)}) %copy-start) | copy-done | bytes 589848
  2.4 0.0 copy-start.1
  2.4 1.0 %copy-done.1 = bf16[512,1,512]{2,0,1:T(8,128)(2,1)S(1)} copy-done((bf16[512,1,512]{2,0,1:T(8,128)(2,1)S(1)}, bf16[512,1,512]{2,0,1:T(8,128)(2,1)}, u32[]{:S(2)}) %copy-start.1) | copy-done | bytes 524312
  3.4 0.0 copy-start.2
  3.4 0.9 %copy-done.2 = bf16[64,576]{1,0:T(8,128)(2,1)S(1)} copy-done((bf16[64,576]{1,0:T(8,128)(2,1)S(1)}, bf16[64,576]{1,0:T(8,128)(2,1)}, u32[]{:S(2)}) %copy-start.2) | copy-done | bytes 73752
  4.3 38.8 %shard_map.59 = (bf16[576,512]{1,0:T(8,128)(2,1)S(1)}, bf16[64,576]{1,0:T(8,128)(2,1)S(1)}) custom-call(bf16[576,512]{1,0:T(8,128)(2,1)S(1)} %bitcast.8, bf16[64,576]{1,0:T(8,128)(2,1)S(1)} %copy-done.2, bf16[512,512]{1,0:T(8,128)(2,1)S(1)} %bitcast.10, s32[1,512]{1,0:T(1,128)S(1)} %bitcast.11), custom_call_target="tpu_custom_call" | custom-call | tf_op jit(solution)/shard_map/pallas_call | solution.py:373
  43.1 0.8 %copy.8 = bf16[512,1,576]{0,2,1:T(8,128)(2,1)} copy(bf16[512,1,576]{0,2,1:T(8,128)(2,1)S(1)} %bitcast.9) | data formatting | bytes 1179648
  43.9 0.6 %copy.9 = bf16[64,576]{1,0:T(8,128)(2,1)} copy(bf16[64,576]{1,0:T(8,128)(2,1)S(1)} %get-tuple-element.9) | data formatting | bytes 147456
Async XLA Ops:
  0.6 0.7 %copy-start.3 = (s32[512]{0:T(512)S(1)}, s32[512]{0:T(512)}, u32[]{:S(2)}) copy-start(s32[512]{0:T(512)} %param.7) | copy-start | bytes 6148
  1.3 1.1 %copy-start = (bf16[512,1,576]{0,2,1:T(8,128)(2,1)S(1)}, bf16[512,1,576]{0,2,1:T(8,128)(2,1)}, u32[]{:S(2)}) copy-start(bf16[512,1,576]{0,2,1:T(8,128)(2,1)} %param.4) | copy-start | bytes 1769476
  2.4 1.0 %copy-start.1 = (bf16[512,1,512]{2,0,1:T(8,128)(2,1)S(1)}, bf16[512,1,512]{2,0,1:T(8,128)(2,1)}, u32[]{:S(2)}) copy-start(bf16[512,1,512]{2,0,1:T(8,128)(2,1)} %param.6) | copy-start | bytes 1572868
  3.4 0.9 %copy-start.2 = (bf16[64,576]{1,0:T(8,128)(2,1)S(1)}, bf16[64,576]{1,0:T(8,128)(2,1)}, u32[]{:S(2)}) copy-start(bf16[64,576]{1,0:T(8,128)(2,1)} %lat_hbm.1) | copy-start | bytes 221188

commit v2 on v1

--- a/solution.py
+++ b/solution.py
@@ -115,32 +115,21 @@
 
 def kernel(
     groups, count, q_hbm, lat_hbm, grad_hbm, first_ref, dq_hbm, dl_ref,
-    q, grad, kv, s, dp, p, ds, dq, acc, own_acc, part, red, prev_part, next_part,
-    in_sem, gat_send, gat_recv, fwd_send, fwd_recv, pp_send, pp_recv, red_send, red_recv, out_sem,
+    q, grad, kv, s, dp, p, ds, dq, acc, keep, pair_part, pair_in, part, red, prev_part, next_part,
+    in_sem, gat_send, hop_send, gat_recv, fwd_send, fwd_recv, pp_send, pp_recv,
+    pair_send, pair_recv, red_send, red_recv, out_sem,
 ):
     width, block = q.shape
     rank = grad.shape[1]
     rows = block // count
     tiles = block // TILE
-    per_tile = TILE // rows
     me = lax.axis_index("blk")
     group = lax.axis_index("grp")
     has_prev = group > 0
     has_next = group < groups - 1
-    my_tile = me // per_tile
+    my_tile, side = me // 2, me % 2
+    neighbour = my_tile * 2 + 1 - side
     prev_tiles = tiles * jnp.minimum(group, 1)
-
-    barrier = pltpu.get_barrier_semaphore()
-    for d in range(1, count):
-        pl.semaphore_signal(barrier, inc=1, device_id={"blk": xor(me, d, count)}, device_id_type=MESH)
-
-    @pl.when(has_prev)
-    def _():
-        pl.semaphore_signal(barrier, inc=1, device_id={"grp": group - 1}, device_id_type=MESH)
-
-    @pl.when(has_next)
-    def _():
-        pl.semaphore_signal(barrier, inc=1, device_id={"grp": group + 1}, device_id_type=MESH)
 
     own_shard = pltpu.make_async_copy(lat_hbm, kv.at[pl.ds(block + me * rows, rows)], in_sem.at[0])
     q_copy = pltpu.make_async_copy(q_hbm, q, in_sem.at[1])
@@ -149,19 +138,49 @@
     q_copy.start()
     grad_copy.start()
 
+    def column(d):
+        return xor(my_tile, d, tiles) * 2 + side
+
+    barrier = pltpu.get_barrier_semaphore()
+    pl.semaphore_signal(barrier, inc=1, device_id={"blk": neighbour}, device_id_type=MESH)
+    for d in range(1, tiles):
+        pl.semaphore_signal(barrier, inc=1, device_id={"blk": column(d)}, device_id_type=MESH)
+
+    @pl.when(has_prev)
+    def _():
+        pl.semaphore_signal(barrier, inc=1, device_id={"grp": group - 1}, device_id_type=MESH)
+
+    @pl.when(has_next)
+    def _():
+        pl.semaphore_signal(barrier, inc=1, device_id={"grp": group + 1}, device_id_type=MESH)
+
+    own_shard.wait()
     if groups == 2:
-        pl.semaphore_wait(barrier, count)
+        pl.semaphore_wait(barrier, tiles + 1)
     else:
         ends = jnp.minimum(group, 1) + jnp.minimum(groups - 1 - group, 1)
-        pl.semaphore_wait(barrier, count - 1 + ends)
-
-    def gather(d, source, target):
-        return pltpu.make_async_remote_copy(
-            src_ref=lat_hbm,
-            dst_ref=kv.at[pl.ds(block + source * rows, rows)],
+        pl.semaphore_wait(barrier, tiles + ends)
+
+    def shard(j):
+        return kv.at[pl.ds(block + j * rows, rows)]
+
+    def spread(d, source, target):
+        return pltpu.make_async_remote_copy(
+            src_ref=shard(source),
+            dst_ref=shard(source),
             send_sem=gat_send.at[d],
             recv_sem=gat_recv.at[source],
             device_id={"blk": target},
+            device_id_type=MESH,
+        )
+
+    def hop(tile, j):
+        return pltpu.make_async_remote_copy(
+            src_ref=shard(j),
+            dst_ref=shard(j),
+            send_sem=hop_send.at[tile],
+            recv_sem=gat_recv.at[j],
+            device_id={"blk": neighbour},
             device_id_type=MESH,
         )
 
@@ -185,19 +204,34 @@
             device_id_type=MESH,
         )
 
+    def pair(tile):
+        return pltpu.make_async_remote_copy(
+            src_ref=pair_part.at[tile],
+            dst_ref=pair_in.at[tile],
+            send_sem=pair_send.at[tile],
+            recv_sem=pair_recv.at[tile],
+            device_id={"blk": neighbour},
+            device_id_type=MESH,
+        )
+
     def reduce(source, target):
         return pltpu.make_async_remote_copy(
-            src_ref=part.at[pl.ds(target * rows, rows)],
+            src_ref=part.at[target],
             dst_ref=red.at[source],
             send_sem=red_send.at[target],
             recv_sem=red_recv.at[source],
-            device_id={"blk": target},
-            device_id_type=MESH,
-        )
-
-    for d in range(count - 1, 0, -1):
-        gather(d, me, xor(me, d, count)).start()
-    own_shard.wait()
+            device_id={"blk": target * 2 + side},
+            device_id_type=MESH,
+        )
+
+    hop(my_tile, me).start()
+    for d in range(1, tiles):
+        spread(d, me, column(d)).start()
+
+    @pl.when(has_next)
+    def _():
+        forward(me, group + 1).start()
+
     q_copy.wait()
     grad_copy.wait()
 
@@ -212,25 +246,35 @@
         dp[at, :] = dot_nt(keys[:, :rank], grad[...])
         return jnp.maximum(largest, jnp.max(tile_s, axis=0, keepdims=True))
 
+    def relay(step):
+        tile = xor(my_tile, step, tiles)
+        j = tile * 2 + side
+        spread(0, j, j).wait_recv()
+        hop(tile, j).start()
+
+        @pl.when(has_next)
+        def _():
+            forward(j, group + 1).start()
+
     def own_scores(step, largest):
+        @pl.when(step + 1 < tiles)
+        def _():
+            relay(step + 1)
+
         tile = xor(my_tile, step, tiles)
-        for sub in range(per_tile):
-            j = tile * per_tile + sub
-
-            @pl.when(j != me)
-            def _():
-                gather(0, j, j).wait_recv()
-
-            @pl.when(has_next)
-            def _():
-                forward(j, group + 1).start()
+        j = tile * 2 + 1 - side
+        hop(tile, j).wait_recv()
+
+        @pl.when(has_next)
+        def _():
+            forward(j, group + 1).start()
 
         return scores_of(block + tile * TILE, tile * TILE + key_in_tile <= token, largest)
 
     def prev_scores(step, largest):
         tile = xor(my_tile, step, tiles)
-        for sub in range(per_tile):
-            forward(tile * per_tile + sub, group - 1).wait_recv()
+        for j in (tile * 2, tile * 2 + 1):
+            forward(j, group - 1).wait_recv()
         position = (group - 1) * block + tile * TILE + key_in_tile
         return scores_of(tile * TILE, position >= first_ref[...], largest)
 
@@ -299,8 +343,19 @@
     def _():
         query_grads()
 
-    def own_latents(step, carry):
-        tile = xor(my_tile, tiles - 1 - step, tiles)
+    def pair_sum(step):
+        tile = xor(my_tile, step, tiles)
+        pair(tile).wait_recv()
+        keep[tile] += pair_in[tile].astype(jnp.float32)
+
+        @pl.when(tile != my_tile)
+        def _():
+            part[tile] = keep[tile].astype(jnp.bfloat16)
+            reduce(my_tile, tile).start()
+
+    def own_latents(i, carry):
+        step = tiles - 1 - i
+        tile = xor(my_tile, step, tiles)
         at = pl.ds(pl.multiple_of(tile * TILE, TILE), TILE)
         latent_terms(block + tile * TILE)
 
@@ -309,17 +364,15 @@
             prev_terms(tile, group + 1).wait_recv()
             acc[...] += next_part[at, :].astype(jnp.float32)
 
-        part[at, :] = acc[...].astype(jnp.bfloat16)
-        for sub in range(per_tile):
-            j = tile * per_tile + sub
-
-            @pl.when(j != me)
-            def _():
-                reduce(me, j).start()
-
-            @pl.when(j == me)
-            def _():
-                own_acc[...] = acc[sub * rows:(sub + 1) * rows, :]
+        theirs = pl.ds(pl.multiple_of((1 - side) * rows, rows), rows)
+        mine = pl.ds(pl.multiple_of(side * rows, rows), rows)
+        pair_part[tile] = acc[theirs, :].astype(jnp.bfloat16)
+        pair(tile).start()
+        keep[tile] = acc[mine, :]
+
+        @pl.when(i > 0)
+        def _():
+            pair_sum(step + 1)
 
         return carry
 
@@ -329,17 +382,21 @@
     def _():
         query_grads()
 
-    total = own_acc[...]
-    for d in range(1, count):
-        source = xor(me, d, count)
-        reduce(source, me).wait_recv()
+    pair_sum(0)
+    total = keep[my_tile]
+    for d in range(1, tiles):
+        source = xor(my_tile, d, tiles)
+        reduce(source, my_tile).wait_recv()
         total = total + red[source].astype(jnp.float32)
     dl_ref[...] = total.astype(dl_ref.dtype)
 
     pltpu.make_async_copy(dq, dq_hbm, out_sem).wait()
-    for d in range(1, count):
-        gather(d, me, xor(me, d, count)).wait_send()
-        reduce(me, xor(me, d, count)).wait_send()
+    for tile in range(tiles):
+        hop(tile, tile * 2 + side).wait_send()
+        pair(tile).wait_send()
+    for d in range(1, tiles):
+        spread(d, me, column(d)).wait_send()
+        reduce(my_tile, xor(my_tile, d, tiles)).wait_send()
 
     @pl.when(has_next)
     def _():
@@ -356,7 +413,7 @@
     rows = block // count
     tiles = block // TILE
     powers = count & (count - 1) == 0 and tiles & (tiles - 1) == 0
-    return head_local == 1 and rows % 16 == 0 and TILE % rows == 0 and block % TILE == 0 and powers
+    return head_local == 1 and rows % 16 == 0 and TILE == 2 * rows and block % TILE == 0 and powers
 
 
 def shards(queries, latents, out_grad, first_key):
@@ -368,7 +425,7 @@
     rows, tiles = block // count, block // TILE
     bf16, f32 = jnp.bfloat16, jnp.float32
     dma = pltpu.SemaphoreType.DMA
-    anywhere = pl.BlockSpec(memory_space=pl.ANY)
+    anywhere = pl.BlockSpec(memory_space=pltpu.HBM)
     vmem = pl.BlockSpec(memory_space=pltpu.VMEM)
     query_grad, latent_grad = pl.pallas_call(
         functools.partial(kernel, groups, count),
@@ -388,24 +445,29 @@
             pltpu.VMEM((2 * block, block), bf16),
             pltpu.VMEM((width, block), bf16),
             pltpu.VMEM((TILE, width), f32),
-            pltpu.VMEM((rows, width), f32),
-            pltpu.VMEM((block, width), bf16),
-            pltpu.VMEM((count, rows, width), bf16),
+            pltpu.VMEM((tiles, rows, width), f32),
+            pltpu.VMEM((tiles, rows, width), bf16),
+            pltpu.VMEM((tiles, rows, width), bf16),
+            pltpu.VMEM((tiles, rows, width), bf16),
+            pltpu.VMEM((tiles, rows, width), bf16),
             pltpu.VMEM((block, width), bf16),
             pltpu.VMEM((block, width), bf16),
             dma((3,)),
+            dma((tiles,)),
+            dma((tiles,)),
             dma((count,)),
             dma((count,)),
             dma((count,)),
-            dma((count,)),
-            dma((tiles,)),
-            dma((tiles,)),
-            dma((count,)),
-            dma((count,)),
+            dma((tiles,)),
+            dma((tiles,)),
+            dma((tiles,)),
+            dma((tiles,)),
+            dma((tiles,)),
+            dma((tiles,)),
             dma,
         ],
         compiler_params=pltpu.CompilerParams(
-            collective_id=0, has_side_effects=True, vmem_limit_bytes=40 * 1024 * 1024
+            collective_id=0, has_side_effects=True, vmem_limit_bytes=63 * 1024 * 1024
         ),
     )(
         queries.reshape(block, width).T,

time: 45.4 us -> 40.9 us (0.901); the launches traced: 44.6 us -> 40.8 us
  local copies, waits for them, and re-layouts: 5.12 us -> 2.59 us
  Pallas kernels: 38.8 us -> 37.5 us
    unnamed x10 -> x4, local copies, waits for them, and re-layouts: 5.12 us -> 2.59 us
    pallas_call x1, Pallas kernels: 38.8 us -> 37.5 us  [shards(): pl.pallas_call(functools.partial(kernel, groups, count), out_shape=(jax.S...]
where the time goes in v2:
time: 40.9 us; the launch traced here: 40.8 us
  Pallas kernels  37.5 us (92%)
  local copies, waits for them, and re-layouts  2.59 us (6%)
  between operations  0.65 us (2%)
    pallas_call x1, Pallas kernels, shards(): pl.pallas_call(functools.partial(kernel, groups, count), out_shape=(jax.S...  37.5 us
    unnamed x4, local copies, waits for them, and re-layouts  2.59 us

profile of v2, /device:TPU:0, one launch (start us, length us, event | category | flops | bytes accessed | tf_op | source)
XLA Modules:
  0.0 40.8 jit_solution(13111350512392168117)
XLA Ops:
  0.6 37.5 %shard_map.59 = (bf16[576,512]{1,0:T(8,128)(2,1)}, bf16[64,576]{1,0:T(8,128)(2,1)}) custom-call(bf16[576,512]{1,0:T(8,128)(2,1)} %bitcast.8, bf16[64,576]{1,0:T(8,128)(2,1)} %lat_hbm.1, bf16[512,512]{1,0:T(8,128)(2,1)} %bitcast.10, s32[1,512]{1,0:T(1,128)} %bitcast.11), custom_call_target="tpu_custom_call" | custom-call | tf_op jit(solution)/shard_map/pallas_call | solution.py:430
  38.2 0.0 copy-start
  38.2 1.9 %copy.8 = bf16[512,1,576]{0,2,1:T(8,128)(2,1)} copy(bf16[512,1,576]{0,2,1:T(8,128)(2,1)} %bitcast.9) | data formatting | bytes 1179648
  40.1 0.0 copy-done
  40.1 0.6 %copy.9 = bf16[64,576]{1,0:T(8,128)(2,1)} copy(bf16[64,576]{1,0:T(8,128)(2,1)S(1)} %copy-done) | data formatting | bytes 147456
Async XLA Ops:
  38.2 2.0 %copy-start = (bf16[64,576]{1,0:T(8,128)(2,1)S(1)}, bf16[64,576]{1,0:T(8,128)(2,1)}, u32[]{:S(2)}) copy-start(bf16[64,576]{1,0:T(8,128)(2,1)} %get-tuple-element.9) | copy-start | bytes 221188

commit v3 on v2

--- a/solution.py
+++ b/solution.py
@@ -115,7 +115,7 @@
 
 def kernel(
     groups, count, q_hbm, lat_hbm, grad_hbm, first_ref, dq_hbm, dl_ref,
-    q, grad, kv, s, dp, p, ds, dq, acc, keep, pair_part, pair_in, part, red, prev_part, next_part,
+    q, grad, kv, s, dp, p, ds, dq, tops, sums, acc, keep, pair_part, pair_in, part, red, prev_part, next_part,
     in_sem, gat_send, hop_send, gat_recv, fwd_send, fwd_recv, pp_send, pp_recv,
     pair_send, pair_recv, red_send, red_recv, out_sem,
 ):
@@ -242,9 +242,13 @@
         at = pl.ds(pl.multiple_of(start, TILE), TILE)
         keys = kv[at, :]
         tile_s = jnp.where(visible, dot_nn(keys, q[...]) * score_scale, HIDDEN)
-        s[at, :] = tile_s
         dp[at, :] = dot_nt(keys[:, :rank], grad[...])
-        return jnp.maximum(largest, jnp.max(tile_s, axis=0, keepdims=True))
+        top = jnp.max(tile_s, axis=0, keepdims=True)
+        e = jnp.exp(tile_s - top)
+        s[at, :] = e
+        tops[start // TILE] = top
+        sums[start // TILE] = jnp.sum(e, axis=0, keepdims=True)
+        return jnp.maximum(largest, top)
 
     def relay(step):
         tile = xor(my_tile, step, tiles)
@@ -285,35 +289,31 @@
     def tile_rows(i):
         return pl.ds(pl.multiple_of(i * TILE, TILE), TILE)
 
-    def exps(i, total):
-        at = tile_rows(i)
-        e = jnp.exp(s[at, :] - largest)
-        s[at, :] = e
-        return total + jnp.sum(e, axis=0, keepdims=True)
+    def rescale(i, total):
+        factor = jnp.exp(tops[i] - largest)
+        tops[i] = factor
+        return total + factor * sums[i]
 
     zero = jnp.zeros((1, block), jnp.float32)
     first_tile = tiles - prev_tiles
-    inverse = 1.0 / lax.fori_loop(first_tile, 2 * tiles, exps, zero)
+    inverse = 1.0 / lax.fori_loop(first_tile, 2 * tiles, rescale, zero)
 
     def probs(i, delta):
         at = tile_rows(i)
-        tile_p = (s[at, :] * inverse).astype(jnp.bfloat16)
+        tile_p = (s[at, :] * (tops[i] * inverse)).astype(jnp.bfloat16)
         p[at, :] = tile_p
         return delta + jnp.sum(tile_p.astype(jnp.float32) * dp[at, :], axis=0, keepdims=True)
 
     delta = lax.fori_loop(first_tile, 2 * tiles, probs, zero)
 
-    def score_grads(i, carry):
-        at = tile_rows(i)
-        ds[at, :] = (p[at, :].astype(jnp.float32) * (dp[at, :] - delta) * score_scale).astype(jnp.bfloat16)
-        return carry
-
-    lax.fori_loop(first_tile, 2 * tiles, score_grads, 0)
+    def score_grads(at):
+        tile_d = p[at, :].astype(jnp.float32) * (dp[at, :] - delta) * score_scale
+        ds[at, :] = tile_d.astype(jnp.bfloat16)
 
     def latent_terms(start):
         at = pl.ds(pl.multiple_of(start, TILE), TILE)
-        d = ds[at, :]
-        acc[...] = dot_nt(d, q[...])
+        score_grads(at)
+        acc[...] = dot_nt(ds[at, :], q[...])
         acc[:, :rank] += dot_nn(p[at, :], grad[...])
 
     def prev_latents(step, carry):
@@ -341,6 +341,8 @@
 
     @pl.when(has_next)
     def _():
+        for i in range(tiles, 2 * tiles):
+            score_grads(pl.ds(i * TILE, TILE))
         query_grads()
 
     def pair_sum(step):
@@ -444,6 +446,8 @@
             pltpu.VMEM((2 * block, block), bf16),
             pltpu.VMEM((2 * block, block), bf16),
             pltpu.VMEM((width, block), bf16),
+            pltpu.VMEM((2 * tiles, 1, block), f32),
+            pltpu.VMEM((2 * tiles, 1, block), f32),
             pltpu.VMEM((TILE, width), f32),
             pltpu.VMEM((tiles, rows, width), f32),
             pltpu.VMEM((tiles, rows, width), bf16),

time: 40.9 us -> 40.4 us (0.988)
  Pallas kernels: 37.5 us -> 37 us
    pallas_call x1, Pallas kernels: 37.5 us -> 37 us  [shards(): pl.pallas_call(functools.partial(kernel, groups, count), out_shape=(jax.S...]
where the time goes in v3:
time: 40.4 us; the launch traced here: 40.2 us
  Pallas kernels  37 us (92%)
  local copies, waits for them, and re-layouts  2.59 us (6%)
  between operations  0.65 us (2%)
    pallas_call x1, Pallas kernels, shards(): pl.pallas_call(functools.partial(kernel, groups, count), out_shape=(jax.S...  37 us
    unnamed x4, local copies, waits for them, and re-layouts  2.59 us

profile of v3, /device:TPU:0, one launch (start us, length us, event | category | flops | bytes accessed | tf_op | source)
XLA Modules:
  0.0 40.2 jit_solution(15732951454243438452)
XLA Ops:
  0.6 37.0 %shard_map.59 = (bf16[576,512]{1,0:T(8,128)(2,1)}, bf16[64,576]{1,0:T(8,128)(2,1)}) custom-call(bf16[576,512]{1,0:T(8,128)(2,1)} %bitcast.8, bf16[64,576]{1,0:T(8,128)(2,1)} %lat_hbm.1, bf16[512,512]{1,0:T(8,128)(2,1)} %bitcast.10, s32[1,512]{1,0:T(1,128)} %bitcast.11), custom_call_target="tpu_custom_call" | custom-call | tf_op jit(solution)/shard_map/pallas_call | solution.py:432
  37.6 0.0 copy-start
  37.6 1.9 %copy.8 = bf16[512,1,576]{0,2,1:T(8,128)(2,1)} copy(bf16[512,1,576]{0,2,1:T(8,128)(2,1)} %bitcast.9) | data formatting | bytes 1179648
  39.6 0.0 copy-done
  39.6 0.6 %copy.9 = bf16[64,576]{1,0:T(8,128)(2,1)} copy(bf16[64,576]{1,0:T(8,128)(2,1)S(1)} %copy-done) | data formatting | bytes 147456
Async XLA Ops:
  37.6 2.0 %copy-start = (bf16[64,576]{1,0:T(8,128)(2,1)S(1)}, bf16[64,576]{1,0:T(8,128)(2,1)}, u32[]{:S(2)}) copy-start(bf16[64,576]{1,0:T(8,128)(2,1)} %get-tuple-element.9) | copy-start | bytes 221188

commit v4 on v3

--- a/solution.py
+++ b/solution.py
@@ -261,9 +261,10 @@
             forward(j, group + 1).start()
 
     def own_scores(step, largest):
-        @pl.when(step + 1 < tiles)
-        def _():
-            relay(step + 1)
+        @pl.when(step == 0)
+        def _():
+            for later in range(1, tiles):
+                relay(later)
 
         tile = xor(my_tile, step, tiles)
         j = tile * 2 + 1 - side
@@ -471,12 +472,12 @@
             dma,
         ],
         compiler_params=pltpu.CompilerParams(
-            collective_id=0, has_side_effects=True, vmem_limit_bytes=63 * 1024 * 1024
+            collective_id=0, has_side_effects=True, vmem_limit_bytes=40 * 1024 * 1024
         ),
     )(
-        queries.reshape(block, width).T,
+        pltpu.with_memory_space_constraint(queries.reshape(block, width).T, pltpu.HBM),
         latents,
-        out_grad.reshape(block, rank),
+        pltpu.with_memory_space_constraint(out_grad.reshape(block, rank), pltpu.HBM),
         first_key.reshape(1, block),
     )
     return (query_grad.T.reshape(block, 1, width), latent_grad)

time: 40.4 us -> 38.7 us (0.958)
  Pallas kernels: 37 us -> 34.9 us
  local copies, waits for them, and re-layouts: 2.59 us -> 3.01 us
    pallas_call x1, Pallas kernels: 37 us -> 34.9 us  [shards(): pl.pallas_call(functools.partial(kernel, groups, count), out_shape=(jax.S...]
    unnamed x4 -> x6, local copies, waits for them, and re-layouts: 2.59 us -> 3.01 us
where the time goes in v4:
time: 38.7 us; the launch traced here: 38.5 us
  Pallas kernels  34.9 us (90%)
  local copies, waits for them, and re-layouts  3.01 us (8%)
  between operations  0.65 us (2%)
    pallas_call x1, Pallas kernels, shards(): pl.pallas_call(functools.partial(kernel, groups, count), out_shape=(jax.S...  34.9 us
    unnamed x6, local copies, waits for them, and re-layouts  3.01 us

profile of v4, /device:TPU:0, one launch (start us, length us, event | category | flops | bytes accessed | tf_op | source)
XLA Modules:
  0.0 38.5 jit_solution(1328384487069865140)
XLA Ops:
  0.6 0.0 copy-start.1
  0.6 0.7 %copy-done.1 = s32[512]{0:T(512)S(1)} copy-done((s32[512]{0:T(512)S(1)}, s32[512]{0:T(512)}, u32[]{:S(2)}) %copy-start.1) | copy-done | bytes 2072
  1.3 0.0 copy-start
  1.3 0.9 %copy-done = bf16[64,576]{1,0:T(8,128)(2,1)S(1)} copy-done((bf16[64,576]{1,0:T(8,128)(2,1)S(1)}, bf16[64,576]{1,0:T(8,128)(2,1)}, u32[]{:S(2)}) %copy-start) | copy-done | bytes 73752
  2.2 34.9 %shard_map.59 = (bf16[576,512]{1,0:T(8,128)(2,1)S(1)}, bf16[64,576]{1,0:T(8,128)(2,1)S(1)}) custom-call(bf16[576,512]{1,0:T(8,128)(2,1)} %bitcast.10, bf16[64,576]{1,0:T(8,128)(2,1)S(1)} %copy-done, bf16[512,512]{1,0:T(8,128)(2,1)} %bitcast.11, s32[1,512]{1,0:T(1,128)S(1)} %bitcast.9), custom_call_target="tpu_custom_call" | custom-call | tf_op jit(solution)/shard_map/pallas_call | solution.py:433
  37.1 0.8 %copy.8 = bf16[512,1,576]{0,2,1:T(8,128)(2,1)} copy(bf16[512,1,576]{0,2,1:T(8,128)(2,1)S(1)} %bitcast.8) | data formatting | bytes 1179648
  37.9 0.6 %copy.9 = bf16[64,576]{1,0:T(8,128)(2,1)} copy(bf16[64,576]{1,0:T(8,128)(2,1)S(1)} %get-tuple-element.9) | data formatting | bytes 147456
Async XLA Ops:
  0.6 0.7 %copy-start.1 = (s32[512]{0:T(512)S(1)}, s32[512]{0:T(512)}, u32[]{:S(2)}) copy-start(s32[512]{0:T(512)} %param.7) | copy-start | bytes 6148
  1.3 0.9 %copy-start = (bf16[64,576]{1,0:T(8,128)(2,1)S(1)}, bf16[64,576]{1,0:T(8,128)(2,1)}, u32[]{:S(2)}) copy-start(bf16[64,576]{1,0:T(8,128)(2,1)} %lat_hbm.1) | copy-start | bytes 221188

commit v5 on v4

--- a/solution.py
+++ b/solution.py
@@ -476,7 +476,7 @@
         ),
     )(
         pltpu.with_memory_space_constraint(queries.reshape(block, width).T, pltpu.HBM),
-        latents,
+        pltpu.with_memory_space_constraint(latents, pltpu.HBM),
         pltpu.with_memory_space_constraint(out_grad.reshape(block, rank), pltpu.HBM),
         first_key.reshape(1, block),
     )

time: 38.7 us -> 37.7 us (0.974)
  local copies, waits for them, and re-layouts: 3.01 us -> 2.13 us
    unnamed x6 -> x4, local copies, waits for them, and re-layouts: 3.01 us -> 2.13 us
where the time goes in v5:
time: 37.7 us; the launch traced here: 37.5 us
  Pallas kernels  34.8 us (92%)
  local copies, waits for them, and re-layouts  2.13 us (6%)
  between operations  0.65 us (2%)
    pallas_call x1, Pallas kernels, shards(): pl.pallas_call(functools.partial(kernel, groups, count), out_shape=(jax.S...  34.8 us
    unnamed x4, local copies, waits for them, and re-layouts  2.13 us

profile of v5, /device:TPU:0, one launch (start us, length us, event | category | flops | bytes accessed | tf_op | source)
XLA Modules:
  0.0 37.5 jit_solution(96155772351044509)
XLA Ops:
  0.6 0.0 copy-start
  0.6 0.7 %copy-done = s32[512]{0:T(512)S(1)} copy-done((s32[512]{0:T(512)S(1)}, s32[512]{0:T(512)}, u32[]{:S(2)}) %copy-start) | copy-done | bytes 2072
  1.3 34.8 %shard_map.59 = (bf16[576,512]{1,0:T(8,128)(2,1)S(1)}, bf16[64,576]{1,0:T(8,128)(2,1)S(1)}) custom-call(bf16[576,512]{1,0:T(8,128)(2,1)} %bitcast.10, bf16[64,576]{1,0:T(8,128)(2,1)} %lat_hbm.1, bf16[512,512]{1,0:T(8,128)(2,1)} %bitcast.11, s32[1,512]{1,0:T(1,128)S(1)} %bitcast.9), custom_call_target="tpu_custom_call" | custom-call | tf_op jit(solution)/shard_map/pallas_call | solution.py:433
  36.1 0.8 %copy.8 = bf16[512,1,576]{0,2,1:T(8,128)(2,1)} copy(bf16[512,1,576]{0,2,1:T(8,128)(2,1)S(1)} %bitcast.8) | data formatting | bytes 1179648
  36.9 0.6 %copy.9 = bf16[64,576]{1,0:T(8,128)(2,1)} copy(bf16[64,576]{1,0:T(8,128)(2,1)S(1)} %get-tuple-element.9) | data formatting | bytes 147456
Async XLA Ops:
  0.6 0.7 %copy-start = (s32[512]{0:T(512)S(1)}, s32[512]{0:T(512)}, u32[]{:S(2)}) copy-start(s32[512]{0:T(512)} %param.7) | copy-start | bytes 6148
